TPU v7x, 256 devices: a whole 4x4x8 slice. The times are simulated.
256 devices in a mesh: lon: 32 (over z, x), lat: 2 (over core), lev: 4 (over y).
Axes of the slice: x: 4, y: 4, z: 8, core: 2. Of those that a mesh axis runs over, the one named last changes fastest.
Arguments:
- state: float32 [6, 8, 1152, 768], P(None, 'lev', 'lon', 'lat'), may hold values from -6 to 6
- east_courant: float32 [8, 1152, 768], P('lev', 'lon', 'lat'), may hold values from -0.2 to 0.2
- north_courant: float32 [8, 1152, 768], P('lev', 'lon', 'lat'), may hold values from -0.2 to 0.2
- cutoff: int32 [768], replicated, may hold values from 4 to 576
Outputs:
- advanced: float32 [6, 8, 1152, 768], P(None, 'lev', 'lon', 'lat')
Inputs may be any that keep to these rules, and one draw needn't show every extreme that they name: `cutoff`: only the entries of the first 96 and the last 96 rows are read.
All inputs are finite; a program needn't handle non-finite values.
Results may differ from a plain program's by a relative error of at most 0.0001.
Values sent between devices are 32-bit elements; how exact they have to be, the bound alone decides.
No kernel may reach another device: no remote copies, remote signals or barrier semaphores. Data moves between devices by JAX's collectives and lax.ppermute only.
A program may use at most 128 MiB of HBM per device.

v0:
```python
import math

import jax
import jax.numpy as jnp
from jax import lax
from jax.sharding import PartitionSpec as P

NLON = 1152
SUBSTEPS = 2


KAPPA = 0.125


def with_halo(cells, sides, width):
    for axis, dim in sides:
        count = lax.axis_size(axis)
        head = lax.slice_in_dim(cells, 0, width, axis=dim)
        tail = lax.slice_in_dim(cells, cells.shape[dim] - width, cells.shape[dim], axis=dim)
        cells = jnp.concatenate(
            [
                lax.ppermute(tail, axis, [(i, (i + 1) % count) for i in range(count)]),
                cells,
                lax.ppermute(head, axis, [((i + 1) % count, i) for i in range(count)]),
            ],
            axis=dim,
        )
    return cells


def passed_along(array, axis, by):
    peers = lax.axis_size(axis)
    return lax.ppermute(array, axis, [(i, (i + by) % peers) for i in range(peers)])


def tables(nlon):
    nwaves = nlon // 2 + 1
    cells = jnp.arange(nlon, dtype=jnp.int32)
    waves = jnp.arange(nwaves, dtype=jnp.int32)
    phase = cells[:, None] * waves[None, :] % nlon
    angle = 2.0 * math.pi / nlon * phase.astype(jnp.float32)
    weight = jnp.where((waves == 0) | (waves == nlon // 2), 1.0, 2.0).astype(jnp.float32) / nlon
    return (jnp.cos(angle), jnp.sin(angle), weight)


def lookup(cutoff, row_ids):
    match = row_ids[:, None] == jnp.arange(cutoff.shape[0], dtype=jnp.int32)[None, :]
    return jnp.sum(jnp.where(match, cutoff[None, :], 0), axis=1)


def filter_circles(block, row_ids, cutoff, costab, sintab, weight):
    share = block.shape[3] // lax.axis_size("lon")
    mine = lax.dynamic_slice_in_dim(row_ids, lax.axis_index("lon") * share, share, 0)
    cuts = lookup(cutoff, mine)
    waves = jnp.arange(weight.shape[0], dtype=jnp.int32)
    keep = jnp.where(waves[None, :] <= cuts[:, None], weight[None, :], 0.0)
    highest = lax.Precision.HIGHEST
    circles = lax.all_to_all(block, "lon", split_axis=3, concat_axis=2, tiled=True)
    cosine = jnp.einsum("flir,ik->flrk", circles, costab, precision=highest)
    sine = jnp.einsum("flir,ik->flrk", circles, sintab, precision=highest)
    result = jnp.einsum("flrk,ik->flir", cosine * keep, costab, precision=highest)
    filtered = result + jnp.einsum("flrk,ik->flir", sine * keep, sintab, precision=highest)
    return lax.all_to_all(filtered, "lon", split_axis=2, concat_axis=3, tiled=True)


def advance(state, east_courant, north_courant, lat_index, global_rows, nlat):
    fields = state.shape[0]
    stacked = jnp.concatenate([state, east_courant[None], north_courant[None]], axis=0)
    padded = with_halo(stacked, (("lon", 2), ("lat", 3)), 1)
    ends = jnp.concatenate([state[:, :, :, :1], state[:, :, :, -1:]], axis=3)
    opposite = passed_along(ends, "lon", lax.axis_size("lon") // 2)
    cells = padded[:fields]
    west = cells[:, :, :-2, 1:-1]
    east = cells[:, :, 2:, 1:-1]
    south = cells[:, :, 1:-1, :-2]
    north = cells[:, :, 1:-1, 2:]
    first_row = jnp.where(lat_index == 0, opposite[:, :, :, :1], south[:, :, :, :1])
    south = jnp.concatenate([first_row, south[:, :, :, 1:]], axis=3)
    last_row = jnp.where(
        lat_index == lax.axis_size("lat") - 1, opposite[:, :, :, 1:], north[:, :, :, -1:]
    )
    north = jnp.concatenate([north[:, :, :, :-1], last_row], axis=3)
    east_face = padded[fields, :, 2:, 1:-1]
    north_face = jnp.where((global_rows == nlat - 1)[None, None, :], 0.0, north_courant)
    south_face = jnp.where((global_rows == 0)[None, None, :], 0.0, padded[fields + 1, :, 1:-1, :-2])
    flux_west = jnp.maximum(east_courant, 0.0) * west + jnp.minimum(east_courant, 0.0) * state
    flux_east = jnp.maximum(east_face, 0.0) * state + jnp.minimum(east_face, 0.0) * east
    flux_south = jnp.maximum(south_face, 0.0) * south + jnp.minimum(south_face, 0.0) * state
    flux_north = jnp.maximum(north_face, 0.0) * state + jnp.minimum(north_face, 0.0) * north
    spread = west + east + south + north - 4.0 * state
    return state + flux_west - flux_east + flux_south - flux_north + KAPPA * spread


def on_device(state, east_courant, north_courant, cutoff):
    lat_dev = state.shape[3]
    polar_count = lat_dev // 4
    n_lat = lax.axis_size("lat")
    nlat = lat_dev * n_lat
    lat_index = lax.axis_index("lat")
    local_rows = jnp.arange(lat_dev, dtype=jnp.int32)
    global_rows = lat_index * lat_dev + local_rows
    polar = (global_rows < polar_count) | (global_rows >= nlat - polar_count)
    costab, sintab, weight = tables(NLON)
    for step in range(SUBSTEPS):
        state = advance(state, east_courant, north_courant, lat_index, global_rows, nlat)
        back = filter_circles(state, global_rows, cutoff, costab, sintab, weight)
        state = jnp.where(polar[None, None, None, :], back, state)
    return state


def solution(mesh):
    return jax.shard_map(
        on_device,
        mesh=mesh,
        in_specs=(
            P(None, "lev", "lon", "lat"),
            P("lev", "lon", "lat"),
            P("lev", "lon", "lat"),
            P(),
        ),
        out_specs=P(None, "lev", "lon", "lat"),
        check_vma=False,
    )
```

profile of v0, /device:TPU:8, one launch (start us, length us, event | category | flops | bytes accessed | tf_op | source)
XLA Modules:
  0.0 482.2 jit_solution(3313576538686688691)
XLA Ops:
  5.3 6.6 %collective-permute-start.1 = (f32[8,2,1,384]{3,0,2,1:T(8,128)S(1)}, f32[8,2,1,384]{3,0,2,1:T(8,128)S(1)}, u32[]{:S(2)}, u32[]{:S(2)}) collective-permute-start(f32[8,2,1,384]{3,0,2,1:T(8,128)S(1)} %get-tuple-element.28), channel_id=1, source_target_pairs={{8,0},{16,8},{24,16},{32,24},{40,32},{48,40},{56,48},{64,56},{72,6... | collective-permute-start | bytes 73736 | tf_op jit(solution)/shard_map/ppermute | solution.py:24
  12.6 4.5 collective-permute-start.3
  21.2 5.0 %copy.217 = f32[6,2,36,383]{2,1,3,0:T(2,128)} copy(f32[6,2,36,383]{3,1,2,0:T(2,128)} %get-tuple-element.31) | data formatting | bytes 1323648 | tf_op jit(solution)/shard_map/slice | solution.py:78
  26.3 3.1 copy.226
  36.1 3.6 copy.284
  44.2 11.1 %add_add_fusion = (f32[6,2,36,384]{2,1,3,0:T(2,128)}, f32[6,2,36,384]{2,1,3,0:T(2,128)}, f32[6,2,36,384]{2,1,3,0:T(2,128)}, f32[6,2,36,384]{2,1,3,0:T(2,128)}) fusion(f32[6,2,36,384]{2,1,3,0:T(2,128)} %copy.284, f32[6,2,36,384]{2,1,3,0:T(2,128)} %copy.285, f32[6,2,36,1]{2,1,3,0:T(2,128)S(1)} %get-tuple-element.42, f32[6,2,36,383]{2,1,3,0:T(2,128)} %copy.226, ...), kind=kLoop, calls=%fused_computation.34 | loop fusion | flops 1327104 | bytes 5640192 | tf_op jit(solution)/shard_map/add | solution.py:90
  55.3 3.7 copy.202
  59.1 3.7 copy.221
  62.9 4.9 %copy.227 = f32[6,2,36,384]{3,1,2,0:T(2,128)} copy(f32[6,2,36,384]{2,1,3,0:T(2,128)} %get-tuple-element.15) | data formatting | bytes 1327104 | tf_op jit(solution)/shard_map/mul | solution.py:89
  67.8 4.9 %copy.229 = f32[6,2,36,384]{3,1,2,0:T(2,128)} copy(f32[6,2,36,384]{2,1,3,0:T(2,128)} %get-tuple-element.13) | data formatting | bytes 1327104 | tf_op jit(solution)/shard_map/add | solution.py:90
  72.7 3.6 subtract_multiply_fusion
  76.4 3.6 copy.231
  80.0 3.1 copy.232
  83.1 2.9 add.125
  88.3 5.4 %reshape.67 = f32[32,1,5184]{2,1,0:T(1,128)} reshape(f32[384,6,2,36]{3,2,1,0:T(2,128)S(1)} %bitcast.115) | data formatting | bytes 1327104
  93.6 4.1 all-to-all-start
  98.1 20.6 %all-to-all-done = f32[32,1,5184]{2,1,0:T(1,128)S(1)} async-done(((f32[32,1,5184]{2,1,0:T(1,128)}), f32[32,1,5184]{2,1,0:T(1,128)S(1)}, u32[]{:S(2)}, u32[]{:S(2)}) %all-to-all-start) | async-done | bytes 663584 | tf_op jit(solution)/shard_map/all_to_all | solution.py:58
  121.5 4.1 reshape.68
  127.8 3.6 reshape.65
  131.4 13.3 %fusion.73 = f32[6,2,12,577]{3,2,1,0:T(8,128)S(1)} fusion(f32[6,2,1152,12]{2,3,1,0:T(8,128)S(1)} %reshape.65, f32[12,577]{1,0:T(8,128)S(1)} %fusion.95), kind=kOutput, calls=%fused_computation.71 | convolution fusion | flops 1154673920 | bytes 1023600 | tf_op jit(solution)/shard_map/flir,ik->flrk/dot_general | solution.py:60
  144.7 13.3 %fusion.67 = f32[6,2,12,577]{3,2,1,0:T(8,128)S(1)} fusion(f32[6,2,1152,12]{2,3,1,0:T(8,128)S(1)} %reshape.65, f32[12,577]{1,0:T(8,128)S(1)} %fusion.95), kind=kOutput, calls=%fused_computation.69 | convolution fusion | flops 1154673920 | bytes 1023600 | tf_op jit(solution)/shard_map/flir,ik->flrk/dot_general | solution.py:59
  158.1 13.7 %fusion.6 = f32[1152,6,2,12]{0,3,2,1:T(8,128)S(1)} fusion(f32[6,2,12,577]{3,2,1,0:T(8,128)S(1)} %fusion.73), kind=kOutput, calls=%fused_computation.7 | convolution fusion | flops 1154590848 | bytes 995904 | tf_op jit(solution)/shard_map/flrk,ik->flir/dot_general | solution.py:62
  171.7 14.0 %fusion.40 = f32[6,2,1152,12]{2,3,1,0:T(8,128)S(1)} fusion(f32[1152,6,2,12]{0,3,2,1:T(8,128)S(1)} %fusion.6, f32[6,2,12,577]{3,2,1,0:T(8,128)S(1)} %fusion.67), kind=kOutput, calls=%fused_computation.28 | convolution fusion | flops 1154756736 | bytes 1659456 | tf_op jit(solution)/shard_map/flrk,ik->flir/dot_general | solution.py:61
  185.7 7.3 %copy.238 = f32[6,2,1152,12]{3,1,0,2:T(2,128)} copy(f32[6,2,1152,12]{2,3,1,0:T(8,128)S(1)} %fusion.40) | data formatting | bytes 1327104 | tf_op jit(solution)/shard_map/add | solution.py:62
  193.1 11.8 %reshape.69 = f32[32,1,5184]{2,1,0:T(1,128)} reshape(f32[1152,6,2,12]{3,2,1,0:T(2,128)} %bitcast.107) | data formatting | bytes 1327104
  204.9 5.2 %all-to-all-start.1 = ((f32[32,1,5184]{2,1,0:T(1,128)}), f32[32,1,5184]{2,1,0:T(1,128)S(1)}, u32[]{:S(2)}, u32[]{:S(2)}) async-start(f32[32,1,5184]{2,1,0:T(1,128)} %reshape.69), calls=%async_computation.1 | async-start | bytes 1343488 | tf_op jit(solution)/shard_map/all_to_all | solution.py:63
  211.9 18.0 %all-to-all-done.1 = f32[32,1,5184]{2,1,0:T(1,128)S(1)} async-done(((f32[32,1,5184]{2,1,0:T(1,128)}), f32[32,1,5184]{2,1,0:T(1,128)S(1)}, u32[]{:S(2)}, u32[]{:S(2)}) %all-to-all-start.1) | async-done | bytes 663584 | tf_op jit(solution)/shard_map/all_to_all | solution.py:63
  232.2 12.9 %reshape.70 = f32[1152,6,2,12]{3,2,1,0:T(2,128)} reshape(f32[32,5184]{1,0:T(8,128)S(1)} %reduce.1) | data formatting | bytes 1327104
  245.0 9.0 %copy.273 = f32[6,2,32,36,12]{3,2,1,4,0:T(8,128)S(1)} copy(f32[6,2,32,36,12]{4,1,0,3,2:T(2,128)} %bitcast.108) | data formatting | bytes 1327104 | tf_op jit(solution)/shard_map/all_to_all | solution.py:63
  259.2 3.4 fusion.126
  264.2 4.2 collective-permute-start.6
  279.9 3.6 copy.291
  287.1 3.6 copy.290
  297.1 11.3 %multiply_add_fusion = f32[6,2,36,384]{2,1,3,0:T(2,128)S(1)} fusion(f32[6,2,36,384]{2,1,3,0:T(2,128)S(1)} %broadcast_select_fusion.1, f32[6,2,36,384]{2,1,3,0:T(2,128)} %copy.290, f32[6,2,36,384]{2,1,3,0:T(2,128)} %copy.291, f32[6,2,36,1]{2,1,3,0:T(2,128)S(1)} %get-tuple-element.40, f32[6,2,36,383]{2,1,3,0:T(2,128)} %get-tuple-element.10, ...), kind=kLoop, calls=%fused_computation.33 | loop fusion | flops 4147200 | bytes 4866048 | tf_op jit(solution)/shard_map/add | solution.py:91
  310.7 4.5 reshape.71
  315.2 26.8 %all_to_all.72 = f32[32,1,5184]{2,1,0:T(1,128)S(1)} all-to-all(f32[32,1,5184]{2,1,0:T(1,128)S(1)} %reshape.71), channel_id=1, replica_groups=mesh['lon'=32,'lat'=2,'lev'=4] {'lon'}, dimensions={0} | all-to-all | bytes 1327104 | tf_op jit(solution)/shard_map/all_to_all | solution.py:58
  344.2 4.1 reshape.72
  350.4 3.4 reshape.66
  353.8 13.4 %fusion.76 = f32[6,2,12,577]{3,2,1,0:T(8,128)S(1)} fusion(f32[6,2,1152,12]{2,3,1,0:T(8,128)S(1)} %reshape.66, f32[12,577]{1,0:T(8,128)S(1)} %fusion.95), kind=kOutput, calls=%fused_computation.72 | convolution fusion | flops 1154673920 | bytes 1023600 | tf_op jit(solution)/shard_map/flir,ik->flrk/dot_general | solution.py:60
  367.2 13.5 %fusion.70 = f32[6,2,12,577]{3,2,1,0:T(8,128)S(1)} fusion(f32[6,2,1152,12]{2,3,1,0:T(8,128)S(1)} %reshape.66, f32[12,577]{1,0:T(8,128)S(1)} %fusion.95), kind=kOutput, calls=%fused_computation.70 | convolution fusion | flops 1154673920 | bytes 1023600 | tf_op jit(solution)/shard_map/flir,ik->flrk/dot_general | solution.py:59
  380.7 13.7 %fusion.2 = f32[1152,6,2,12]{0,3,2,1:T(8,128)S(1)} fusion(f32[6,2,12,577]{3,2,1,0:T(8,128)S(1)} %fusion.76), kind=kOutput, calls=%fused_computation.3 | convolution fusion | flops 1154590848 | bytes 995904 | tf_op jit(solution)/shard_map/flrk,ik->flir/dot_general | solution.py:62
  394.4 13.8 %fusion.37 = f32[6,2,1152,12]{2,3,1,0:T(8,128)S(1)} fusion(f32[1152,6,2,12]{0,3,2,1:T(8,128)S(1)} %fusion.2, f32[6,2,12,577]{3,2,1,0:T(8,128)S(1)} %fusion.70), kind=kOutput, calls=%fused_computation.27 | convolution fusion | flops 1154756736 | bytes 1659456 | tf_op jit(solution)/shard_map/flrk,ik->flir/dot_general | solution.py:61
  408.2 7.3 %copy.262 = f32[6,2,1152,12]{3,1,0,2:T(2,128)} copy(f32[6,2,1152,12]{2,3,1,0:T(8,128)S(1)} %fusion.37) | data formatting | bytes 1327104 | tf_op jit(solution)/shard_map/add | solution.py:62
  415.5 11.1 %reshape.73 = f32[32,1,5184]{2,1,0:T(1,128)S(1)} reshape(f32[1152,6,2,12]{3,2,1,0:T(2,128)} %bitcast.109) | data formatting | bytes 1327104
  426.6 24.6 %all_to_all.73 = f32[32,1,5184]{2,1,0:T(1,128)S(1)} all-to-all(f32[32,1,5184]{2,1,0:T(1,128)S(1)} %reshape.73), channel_id=1, replica_groups=mesh['lon'=32,'lat'=2,'lev'=4] {'lon'}, dimensions={0} | all-to-all | bytes 1327104 | tf_op jit(solution)/shard_map/all_to_all | solution.py:63
  453.5 12.9 %reshape.74 = f32[1152,6,2,12]{3,2,1,0:T(2,128)} reshape(f32[32,5184]{1,0:T(8,128)S(1)} %reduce.3) | data formatting | bytes 1327104
  466.4 9.0 %copy.279 = f32[6,2,32,36,12]{3,2,1,4,0:T(8,128)S(1)} copy(f32[6,2,32,36,12]{4,1,0,3,2:T(2,128)} %bitcast.110) | data formatting | bytes 1327104 | tf_op jit(solution)/shard_map/all_to_all | solution.py:63
  479.2 2.7 copy.265
  (126 shorter events, 73.7 us)
Async XLA Ops:
  0.0 11.9 %copy-start.4 = (f32[6,2,36,384]{3,1,2,0:T(2,128)S(1)}, f32[6,2,36,384]{3,1,2,0:T(2,128)}, u32[]{:S(2)}) copy-start(f32[6,2,36,384]{3,1,2,0:T(2,128)} %param.4) | copy-start | bytes 1990660
  0.0 17.1 %copy-start.12 = (f32[2,36,384]{2,0,1:T(2,128)S(1)}, f32[2,36,384]{2,0,1:T(2,128)}, u32[]{:S(2)}) copy-start(f32[2,36,384]{2,0,1:T(2,128)} %param.5) | copy-start | bytes 331780
  3.7 16.4 %copy-start.13 = (f32[2,36,384]{2,0,1:T(2,128)S(1)}, f32[2,36,384]{2,0,1:T(2,128)}, u32[]{:S(2)}) copy-start(f32[2,36,384]{2,0,1:T(2,128)} %param.6) | copy-start | bytes 331780
  3.7 25.7 %collective-permute-start = (f32[8,2,1,384]{3,0,2,1:T(8,128)S(1)}, f32[8,2,1,384]{3,0,2,1:T(8,128)S(1)}, u32[]{:S(2)}, u32[]{:S(2)}) collective-permute-start(f32[8,2,1,384]{3,0,2,1:T(8,128)S(1)} %get-tuple-element.27), channel_id=1, source_target_pairs={{0,8},{8,16},{16,24},{24,32},{32,40},{40,48},{48,56},{56,64},{64,7... | collective-permute-start | bytes 73736 | tf_op jit(solution)/shard_map/ppermute | solution.py:22
  5.3 24.1 %collective-permute-start.1 = (f32[8,2,1,384]{3,0,2,1:T(8,128)S(1)}, f32[8,2,1,384]{3,0,2,1:T(8,128)S(1)}, u32[]{:S(2)}, u32[]{:S(2)}) collective-permute-start(f32[8,2,1,384]{3,0,2,1:T(8,128)S(1)} %get-tuple-element.28), channel_id=1, source_target_pairs={{8,0},{16,8},{24,16},{32,24},{40,32},{48,40},{56,48},{64,56},{72,6... | collective-permute-start | bytes 73736 | tf_op jit(solution)/shard_map/ppermute | solution.py:24
  12.6 30.8 %collective-permute-start.3 = (f32[6,2,36,2]{2,1,3,0:T(2,128)S(1)}, f32[6,2,36,2]{2,1,3,0:T(2,128)}, u32[]{:S(2)}, u32[]{:S(2)}) collective-permute-start(f32[6,2,36,2]{2,1,3,0:T(2,128)S(1)} %pad_maximum_fusion.28), channel_id=1, source_target_pairs={{0,128},{8,136},{16,144},{24,152},{32,160},{40,168},{48,176},{56,1... | collective-permute-start | bytes 10376 | tf_op jit(solution)/shard_map/ppermute | solution.py:33
  20.8 19.9 %copy-start.17 = (pred[384]{0:T(512)(128)(4,1)}, pred[384]{0:T(512)(128)(4,1)S(1)}, u32[]{:S(2)}) copy-start(pred[384]{0:T(512)(128)(4,1)S(1)} %fusion.98) | copy-start | bytes 1156
  21.0 23.2 %copy-start.5 = (f32[2,36,384]{1,0,2:T(2,128)}, f32[2,36,384]{1,0,2:T(2,128)S(1)}, u32[]{:S(2)}) copy-start(f32[2,36,384]{1,0,2:T(2,128)S(1)} %copy.224) | copy-start | bytes 331780
  21.2 23.0 %copy-start.6 = (f32[2,36,384]{1,0,2:T(2,128)}, f32[2,36,384]{1,0,2:T(2,128)S(1)}, u32[]{:S(2)}) copy-start(f32[2,36,384]{1,0,2:T(2,128)S(1)} %copy.195) | copy-start | bytes 331780
  30.0 9.7 %collective-permute-start.2 = (f32[8,2,38,1]{2,1,3,0:T(2,128)S(1)}, f32[8,2,38,1]{2,1,3,0:T(2,128)S(1)}, u32[]{:S(2)}, u32[]{:S(2)}) collective-permute-start(f32[8,2,38,1]{2,1,3,0:T(2,128)S(1)} %copy.286), channel_id=1, source_target_pairs={{0,4},{4,0},{1,5},{5,1},{2,6},{6,2},{3,7},{7,3},{8,12},{12,8},{9,1... | collective-permute-start | bytes 7304 | tf_op jit(solution)/shard_map/ppermute | solution.py:22
  30.3 13.1 %collective-permute-start.4 = (f32[8,2,38,1]{2,1,3,0:T(2,128)S(1)}, f32[8,2,38,1]{2,1,3,0:T(2,128)S(1)}, u32[]{:S(2)}, u32[]{:S(2)}) collective-permute-start(f32[8,2,38,1]{2,1,3,0:T(2,128)S(1)} %copy.289), channel_id=1, source_target_pairs={{4,0},{0,4},{5,1},{1,5},{6,2},{2,6},{7,3},{3,7},{12,8},{8,12},{13,... | collective-permute-start | bytes 7304 | tf_op jit(solution)/shard_map/ppermute | solution.py:24
  62.8 9.8 %copy-start.11 = (f32[1,2,36,384]{3,0,2,1:T(1,128)S(1)}, f32[1,2,36,384]{3,0,2,1:T(1,128)}, u32[]{:S(2)}) copy-start(f32[1,2,36,384]{3,0,2,1:T(1,128)} %get-tuple-element.7) | copy-start | bytes 331780
  62.9 9.9 %copy-start.8 = (f32[2,36,384]{2,0,1:T(2,128)S(1)}, f32[2,36,384]{2,0,1:T(2,128)}, u32[]{:S(2)}) copy-start(f32[2,36,384]{2,0,1:T(2,128)} %get-tuple-element.37) | copy-start | bytes 331780
  62.9 9.9 %copy-start.9 = (f32[2,36,384]{2,0,1:T(2,128)S(1)}, f32[2,36,384]{2,0,1:T(2,128)}, u32[]{:S(2)}) copy-start(f32[2,36,384]{2,0,1:T(2,128)} %get-tuple-element.35) | copy-start | bytes 331780
  76.4 3.6 copy-start.7
  85.9 1.5 copy-start
  88.2 9.6 %copy-start.14 = (s32[768]{0:T(1024)S(1)}, s32[768]{0:T(1024)}, u32[]{:S(2)}) copy-start(s32[768]{0:T(1024)} %param.7) | copy-start | bytes 9220
  93.6 25.1 %all-to-all-start = ((f32[32,1,5184]{2,1,0:T(1,128)}), f32[32,1,5184]{2,1,0:T(1,128)S(1)}, u32[]{:S(2)}, u32[]{:S(2)}) async-start(f32[32,1,5184]{2,1,0:T(1,128)} %reshape.67), calls=%async_computation | async-start | bytes 1343488 | tf_op jit(solution)/shard_map/all_to_all | solution.py:58
  193.1 17.0 %copy-start.10 = (f32[2,36,384]{2,0,1:T(2,128)S(1)}, f32[2,36,384]{2,0,1:T(2,128)}, u32[]{:S(2)}) copy-start(f32[2,36,384]{2,0,1:T(2,128)} %get-tuple-element.35) | copy-start | bytes 331780
  204.9 25.0 %all-to-all-start.1 = ((f32[32,1,5184]{2,1,0:T(1,128)}), f32[32,1,5184]{2,1,0:T(1,128)S(1)}, u32[]{:S(2)}, u32[]{:S(2)}) async-start(f32[32,1,5184]{2,1,0:T(1,128)} %reshape.69), calls=%async_computation.1 | async-start | bytes 1343488 | tf_op jit(solution)/shard_map/all_to_all | solution.py:63
  254.1 1.9 copy-start.1
  254.1 1.9 copy-start.15
  262.9 8.4 %collective-permute-start.5 = (f32[8,2,1,384]{3,0,2,1:T(8,128)S(1)}, f32[8,2,1,384]{3,0,2,1:T(8,128)S(1)}, u32[]{:S(2)}, u32[]{:S(2)}) collective-permute-start(f32[8,2,1,384]{3,0,2,1:T(8,128)S(1)} %get-tuple-element.26), channel_id=1, source_target_pairs={{0,8},{8,16},{16,24},{24,32},{32,40},{40,48},{48,56},{56,64},{64,7... | collective-permute-start | bytes 73736 | tf_op jit(solution)/shard_map/ppermute | solution.py:22
  264.2 7.2 %collective-permute-start.6 = (f32[8,2,1,384]{3,0,2,1:T(8,128)S(1)}, f32[8,2,1,384]{3,0,2,1:T(8,128)S(1)}, u32[]{:S(2)}, u32[]{:S(2)}) collective-permute-start(f32[8,2,1,384]{3,0,2,1:T(8,128)S(1)} %get-tuple-element.25), channel_id=1, source_target_pairs={{8,0},{16,8},{24,16},{32,24},{40,32},{48,40},{56,48},{64,56},{72,6... | collective-permute-start | bytes 73736 | tf_op jit(solution)/shard_map/ppermute | solution.py:24
  268.9 27.3 %collective-permute-start.8 = (f32[6,2,36,2]{2,1,3,0:T(2,128)}, f32[6,2,36,2]{2,1,3,0:T(2,128)}, u32[]{:S(2)}, u32[]{:S(2)}) collective-permute-start(f32[6,2,36,2]{2,1,3,0:T(2,128)} %pad_maximum_fusion.29), channel_id=1, source_target_pairs={{0,128},{8,136},{16,144},{24,152},{32,160},{40,168},{48,176},{56,1... | collective-permute-start | bytes 10376 | tf_op jit(solution)/shard_map/ppermute | solution.py:33
  274.3 16.4 %collective-permute-start.7 = (f32[8,2,38,1]{2,1,3,0:T(2,128)}, f32[8,2,38,1]{2,1,3,0:T(2,128)}, u32[]{:S(2)}, u32[]{:S(2)}) collective-permute-start(f32[8,2,38,1]{2,1,3,0:T(2,128)} %copy.292), channel_id=1, source_target_pairs={{0,4},{4,0},{1,5},{5,1},{2,6},{6,2},{3,7},{7,3},{8,12},{12,8},{9,1... | collective-permute-start | bytes 7304 | tf_op jit(solution)/shard_map/ppermute | solution.py:22
  276.1 20.2 %collective-permute-start.9 = (f32[8,2,38,1]{2,1,3,0:T(2,128)}, f32[8,2,38,1]{2,1,3,0:T(2,128)}, u32[]{:S(2)}, u32[]{:S(2)}) collective-permute-start(f32[8,2,38,1]{2,1,3,0:T(2,128)} %copy.293), channel_id=1, source_target_pairs={{4,0},{0,4},{5,1},{1,5},{6,2},{2,6},{7,3},{3,7},{12,8},{8,12},{13,... | collective-permute-start | bytes 7304 | tf_op jit(solution)/shard_map/ppermute | solution.py:24
  308.4 1.5 copy-start.2
  475.4 1.9 copy-start.3
  475.4 1.9 copy-start.16
where the time goes:
time: 489 us; the launch traced here: 482 us
  local copies, waits for them, and re-layouts  195 us (40%)
  matrix products  109 us (22%)
  other arithmetic  56.5 us (12%)
  blocking collectives  51.4 us (11%)
  waiting for transfers between devices  38.6 us (8%)
  starting transfers between devices  31.1 us (6%)
    unnamed x56, local copies, waits for them, and re-layouts  89.3 us
    dot_general x2, matrix products, filter_circles(): jnp.einsum('flrk,ik->flir', cosine * keep, costab, precision=highest)  27.8 us
    dot_general x2, matrix products, filter_circles(): jnp.einsum('flrk,ik->flir', sine * keep, sintab, precision=highest)  27.3 us
    dot_general x2, matrix products, filter_circles(): cosine = jnp.einsum('flir,ik->flrk', circles, costab, precision=highest)  26.8 us
    all_to_all x1, blocking collectives, filter_circles(): lax.all_to_all(block, 'lon', split_axis=3, concat_axis=2, tiled=True)  26.8 us
    dot_general x2, matrix products, filter_circles(): sine = jnp.einsum('flir,ik->flrk', circles, sintab, precision=highest)  26.7 us
    all_to_all x1, blocking collectives, filter_circles(): lax.all_to_all(filtered, 'lon', split_axis=2, concat_axis=3, tiled=True)  24.6 us
    all_to_all x4, local copies, waits for them, and re-layouts, filter_circles(): lax.all_to_all(filtered, 'lon', split_axis=2, concat_axis=3, tiled=True)  21.7 us
  transfers between devices with their start and end apart: 12, of which 2 were waited for; matrix products, arithmetic and copies ran while one was open for 11% of the time, Pallas kernels for 0%

commit v1 on v0

v1 whole, which is shorter than its diff:
```python
import math

import jax
import jax.numpy as jnp
import numpy as np
from jax import lax
from jax.experimental import pallas as pl
from jax.experimental.layout import Layout, with_layout_constraint
from jax.experimental.pallas import tpu as pltpu
from jax.sharding import PartitionSpec as P

FIELDS = 6
UNITS = 8
NLON = 1152
HALF = NLON // 2
QUARTER = NLON // 4
NLAT = 768
POLAR = 96
LEVELS = 2
LON = 36
LAT = 384
RING = 32
GROUPS = 16
SHARE = 6
SPAN = 10
SLOT = 7
KAPPA = 0.125
BLOCK = 64
PIECE = 48
TILES = LAT // 128
STEP = TILES * LEVELS
UNIT = LON * STEP
EDGE = 2 * STEP + 2 * LEVELS
ORDER = Layout(major_to_minor=(0, 1, 3, 2, 4))


def lanes_of(rows, width=128):
    return lax.broadcasted_iota(jnp.int32, (rows, width), 1)


def pick(flag, rows, width, yes, no):
    return jnp.where(jnp.full((rows, width), flag, jnp.int32) == 0, yes, no)


def to_rows(x):
    units = x.size // (LEVELS * LON * LAT)
    x = x.reshape(units, LEVELS, LON, LAT).transpose(0, 2, 1, 3)
    x = with_layout_constraint(x.reshape(units, LON, LEVELS, TILES, 128), ORDER)
    return x.transpose(0, 1, 3, 2, 4).reshape(units * UNIT, 128)


def from_rows(x):
    x = x.reshape(FIELDS, LON, TILES, LEVELS, 128).transpose(0, 1, 3, 2, 4)
    x = with_layout_constraint(x, ORDER)
    return x.reshape(FIELDS, LON, LEVELS, LAT).transpose(0, 2, 1, 3)


def unit(state, cx, cy, u):
    return (state, u * UNIT) if u < FIELDS else ((cx, cy)[u - FIELDS], 0)


def part(ref, start, level, tile, first, count):
    return ref[pl.ds(start + first * STEP + tile * LEVELS + level, count, stride=STEP), :]


def on_core(body):
    lat = lax.axis_index("lat")
    for n in range(2):
        pl.when(lat == n)(lambda n=n: body(n))


def pack_kernel(state, cx, cy, chunks_out, window_out, edge_out, block, tails, slots, chunks, window, edge, sems):
    loads = []
    for u in range(UNITS):
        ref, start = unit(state, cx, cy, u)
        loads.append(pltpu.make_async_copy(ref.at[start:start + UNIT], block.at[u * UNIT:u * UNIT + UNIT], sems.at[u]))
    for copy in loads:
        copy.start()
    sends = [
        pltpu.make_async_copy(window, window_out, sems.at[UNITS]),
        pltpu.make_async_copy(edge, edge_out, sems.at[UNITS + 1]),
    ]
    for n in range(4):
        some = pl.ds(n * RING // 4, RING // 4)
        sends.append(pltpu.make_async_copy(chunks.at[some], chunks_out.at[some], sems.at[UNITS + 2 + n]))
    lane = lanes_of(8)

    def body(lat):
        for u in range(UNITS):
            loads[u].wait()
            start = u * UNIT
            edge[EDGE * u:EDGE * u + EDGE] = block[start:start + EDGE]
            at = EDGE * (UNITS + u)
            edge[at:at + 12] = block[start + UNIT - 12:start + UNIT]
            edge[at + 12:at + EDGE] = block[start + UNIT - 4:start + UNIT]
            for level in range(LEVELS):
                rows = pl.ds(2 * LON * u + level, LON, stride=LEVELS)
                window[rows, :] = part(block, start, level, 2 - 2 * lat, 0, LON)
                main = part(block, start, level, 2 * lat, 0, 24)
                slots[level, u] = pltpu.roll(main, (SPAN * u - 32 * lat) % 128, 1)
                row = 12 * (u // 4)
                tails[level, u % 4, row:row + 12] = part(block, start, level, 2 * lat, 24, 12)
        sends[0].start()
        sends[1].start()
        for level in range(LEVELS):
            for at in range(4):
                slots[level, 8 + at] = pltpu.roll(tails[level, at], (SPAN * (8 + at) - 32 * lat) % 128, 1)
            for g in range(GROUPS):
                first = SHARE * g - 2
                begins = sorted(((first + SPAN * n) % 128, n) for n in range(12))
                for k in range(0, 24, 8):
                    value = slots[level, begins[-1][1], k:k + 8]
                    for begin, n in begins:
                        value = jnp.where(lane >= begin, slots[level, n, k:k + 8], value)
                    chunks[level * GROUPS + g, k:k + 8] = value
                if g % 8 == 7:
                    sends[2 + level * 2 + g // 8].start()

    on_core(body)
    for copy in sends:
        copy.wait()


def edge_kernel(edge, window, head, tail):
    head[...] = edge[:EDGE * UNITS]
    tail[...] = edge[EDGE * UNITS:]
    for u in range(UNITS):
        at, beyond = EDGE * u, 2 * LON * u
        head[at + 12:at + EDGE] = window[beyond:beyond + 4]
        tail[at + 12:at + EDGE] = window[beyond + 2 * LON - 4:beyond + 2 * LON]


def limit_kernel(head, table, cutoff, limits):
    del head, table
    low = lax.axis_index("lat") * (NLAT - POLAR) + SHARE * lax.rem(lax.axis_index("lon"), GROUPS) - 2
    row = lanes_of(8) % SPAN
    found = jnp.zeros((8, 128), jnp.int32)
    for r in range(SPAN):
        found = jnp.where(row == r, cutoff[jnp.clip(low + r, 0, NLAT - 1)], found)
    limits[...] = found


def coefficients(cx, cx_east, cy_south, cy_north):
    west = jnp.maximum(cx, 0.0) + KAPPA
    east = KAPPA - jnp.minimum(cx_east, 0.0)
    south = jnp.maximum(cy_south, 0.0) + KAPPA
    north = KAPPA - jnp.minimum(cy_north, 0.0)
    centre = (
        (1.0 - 4.0 * KAPPA)
        + (jnp.minimum(cx, 0.0) - jnp.maximum(cx_east, 0.0))
        + (jnp.minimum(cy_south, 0.0) - jnp.maximum(cy_north, 0.0))
    )
    return west, east, south, north, centre


def middle_kernel(state, cx, cy, west, east, window, out, weight, ext, coef):
    lat = lax.axis_index("lat")

    def extended(u, level):
        ref, start = unit(state, cx, cy, u)
        for t in range(TILES):
            ext[:LON, 128 * t:128 * t + 128] = part(ref, start, level, t, 0, LON)
            ext[LON:LON + 2, 128 * t:128 * t + 128] = part(east, EDGE * u, level, t, 0, 2)
            ext[LON + 2:, 128 * t:128 * t + 128] = part(west, EDGE * u, level, t, 0, 2)
        ext[:LON, LAT:] = window[pl.ds(2 * LON * u + level, LON, stride=LEVELS), :]
        ext[LON:LON + 2, LAT:] = east[pl.ds(EDGE * u + 12 + level, 2, stride=LEVELS), :]
        ext[LON + 2:, LAT:] = west[pl.ds(EDGE * u + 12 + level, 2, stride=LEVELS), :]
        return ext[...]

    lane = lanes_of(LON + 4, LAT + 128)
    edge = lane == jnp.where(lat == 0, POLAR - 1, LAT - POLAR)
    beside = lanes_of(LON + 4) == jnp.where(lat == 0, POLAR, 31)
    for level in range(LEVELS):
        cxe = extended(FIELDS, level)
        cye = extended(FIELDS + 1, level)
        parts = coefficients(cxe, pltpu.roll(cxe, LON + 3, 0), pltpu.roll(cye, 1, 1), cye)
        for n, value in enumerate(parts):
            coef[n] = value
        near = pick(lat, LON + 4, 128, parts[2][:, :128], parts[3][:, 256:LAT])
        weight[level * (LON + 4):(level + 1) * (LON + 4)] = jnp.where(beside, near, 0.0)

        def substep(q):
            return (
                coef[0] * pltpu.roll(q, 1, 0)
                + coef[1] * pltpu.roll(q, LON + 3, 0)
                + coef[2] * pltpu.roll(q, 1, 1)
                + coef[3] * pltpu.roll(q, LAT + 127, 1)
                + coef[4] * q
            )

        for u in range(FIELDS):
            once = jnp.where(edge, 0.0, substep(extended(u, level)))
            twice = substep(once)
            for t in range(TILES):
                rows = pl.ds(u * UNIT + t * LEVELS + level, LON, stride=STEP)
                out[rows, :] = twice[:LON, 128 * t:128 * t + 128]


def hartley_tables():
    def split(n, shift):
        at = 2 * np.arange(n, dtype=np.int64) + shift
        angle = 2.0 * np.pi / (4 * n) * (at[:, None] * at[None, :] % (4 * n))
        table = np.cos(angle) + np.sin(angle)
        high = table.astype(jnp.bfloat16)
        low = (table - high.astype(np.float64)).astype(jnp.bfloat16)
        return np.concatenate([high, low], axis=1)

    even = np.concatenate([split(QUARTER, 0), split(QUARTER, 1)], axis=0)
    return np.concatenate([split(HALF, 1), even], axis=1)


def circle_kernel(chunks, table, limits, west, east, out, back, q0, q1, coef, spread, *buffers):
    del west, east
    odd_in, even_in, rest_in, odd_out, even_out, rest_out, lanes_in, sems = buffers
    lat = lax.axis_index("lat")
    group = lax.rem(lax.axis_index("lon"), GROUPS)
    low = SHARE * group - 2
    lane24 = lanes_of(24)
    for i in range(RING):
        chunk = chunks[i]
        at = 8 + LON * i
        q0[at:at + 24] = pltpu.roll(chunk, (-low) & 127, 1)
        upper = pltpu.roll(chunk, (-low - 8 * SPAN) & 127, 1)
        lower = pltpu.roll(chunk, (-low - 4 * SPAN) & 127, 1)
        q0[at + 24:at + 36] = jnp.where(lane24[:12] < 4 * SPAN, upper[:12], lower[12:])
    q0[7:8] = q0[7 + NLON:8 + NLON]
    q0[8 + NLON:9 + NLON] = q0[8:9]

    row = lanes_of(BLOCK) % SPAN
    pole_south = (row == 2) & (jnp.full((BLOCK, 128), lat + group, jnp.int32) == 0)
    pole_north = (row == SPAN - 3) & (jnp.full((BLOCK, 128), lat * GROUPS + group, jnp.int32) == 2 * GROUPS - 1)

    def split(ref, at, x, again=0):
        rows = x.shape[0]
        high = x.astype(jnp.bfloat16)
        rest = (x - high.astype(jnp.float32)).astype(jnp.bfloat16)
        for begin in (at, at + again)[:2 if again else 1]:
            ref[begin:begin + rows, :128] = high
            ref[begin:begin + rows, 128:] = rest

    def moved(sources):
        at = lax.broadcasted_iota(jnp.int32, (128, 128), 0)
        places = [jnp.where(at == source, 1.0, 0.0).astype(jnp.bfloat16) for source in sources]
        places = jnp.concatenate(places, axis=1)
        return jnp.dot(lanes_in[...], jnp.concatenate([places] * 2, axis=0), preferred_element_type=jnp.float32)

    for b in range(0, NLON, PIECE):
        split(lanes_in, b, q0[8 + b:8 + b + PIECE])
    take_x = FIELDS * SPAN + lanes_of(128) % SPAN
    spread[:NLON] = moved((take_x, take_x + SPAN))
    spread[NLON:NLON + 8] = spread[:8]

    def substep(q, b, parts):
        across = q[8 + (b + HALF) % NLON:8 + (b + HALF) % NLON + BLOCK]
        here = q[8 + b:8 + b + BLOCK]
        return (
            parts[0] * q[7 + b:7 + b + BLOCK]
            + parts[1] * q[9 + b:9 + b + BLOCK]
            + parts[2] * jnp.where(pole_south, across, pltpu.roll(here, 1, 1))
            + parts[3] * jnp.where(pole_north, across, pltpu.roll(here, 127, 1))
            + parts[4] * here
        )

    for b in range(0, NLON, BLOCK):
        cy = spread[b:b + BLOCK, 128:]
        parts = coefficients(
            spread[b:b + BLOCK, :128],
            spread[b + 1:b + 1 + BLOCK, :128],
            jnp.where(pole_south, 0.0, pltpu.roll(cy, 1, 1)),
            jnp.where(pole_north, 0.0, cy),
        )
        for n, value in enumerate(parts):
            coef[n, b:b + BLOCK] = value
        q1[8 + b:8 + b + BLOCK] = substep(q0, b, parts)

    limit = limits[:1]

    def kept(at, step, shift):
        wave = step * (lax.broadcasted_iota(jnp.int32, (PIECE, 128), 0) + at) + shift
        return jnp.where(jnp.minimum(wave, NLON - wave) <= limit, 1.0 / NLON, 0.0)

    def products():
        odd_out[...] = jnp.dot(table[:, :NLON], odd_in[...], preferred_element_type=jnp.float32)
        even_out[...] = jnp.dot(table[:QUARTER, NLON:], even_in[...], preferred_element_type=jnp.float32)
        rest_out[...] = jnp.dot(table[QUARTER:, NLON:], rest_in[...], preferred_element_type=jnp.float32)

    def result(ref, at):
        return ref[at:at + PIECE, :128] + ref[at:at + PIECE, 128:]

    def filtered(q, finish):
        for b in range(0, QUARTER, PIECE):
            x = [q[8 + QUARTER * n + b:8 + QUARTER * n + b + PIECE] for n in range(4)]
            split(odd_in, b, x[0] - x[2], HALF)
            split(odd_in, QUARTER + b, x[1] - x[3], HALF)
            here, there = x[0] + x[2], x[1] + x[3]
            split(even_in, b, here + there, QUARTER)
            split(rest_in, b, here - there, QUARTER)
        products()
        for b in range(0, HALF, PIECE):
            split(odd_in, b, result(odd_out, b) * kept(b, 2, 1), HALF)
        for b in range(0, QUARTER, PIECE):
            split(even_in, b, result(even_out, b) * kept(b, 4, 0), QUARTER)
            split(rest_in, b, result(rest_out, b) * kept(b, 4, 2), QUARTER)
        products()
        for b in range(0, QUARTER, PIECE):
            odd = result(odd_out, b), result(odd_out, QUARTER + b)
            even, rest = result(even_out, b), result(rest_out, b)
            both = even + rest, even - rest
            for n in range(2):
                finish(QUARTER * n + b, both[n] + odd[n])
                finish(HALF + QUARTER * n + b, both[n] - odd[n])

    place = low + lanes_of(PIECE) % SPAN
    polar = (place >= 0) & (place < POLAR)

    def finish_first(at, value):
        q1[8 + at:8 + at + PIECE] = jnp.where(polar, value, q1[8 + at:8 + at + PIECE])

    upper = lanes_of(PIECE) >= 64

    def finish_second(at, value):
        before = pltpu.roll(q1[8 + at:8 + at + PIECE], 64, 1)
        split(lanes_in, at, jnp.where(upper, before, value))

    filtered(q1, finish_first)
    q1[7:8] = q1[7 + NLON:8 + NLON]
    q1[8 + NLON:9 + NLON] = q1[8:9]
    for b in range(0, NLON, BLOCK):
        q0[8 + b:8 + b + BLOCK] = substep(q1, b, [coef[n, b:b + BLOCK] for n in range(5)])
    filtered(q0, finish_second)
    spot = (lanes_of(128) - (SHARE * group + 31 * lat)) & 127
    field, r = spot // SLOT, spot % SLOT - lat
    source = field * SPAN + jnp.where((r >= 0) & (r < SHARE), 2 + r, 64 + jnp.where(lat == 0, SPAN - 3, 2))
    q1[8:8 + NLON] = moved((jnp.where(field < FIELDS, source, -1),))
    third = ((lane24 - (SHARE * group + 31 * lat)) & 127) // (FIELDS * SLOT)
    sends = []
    for n in range(RING // 2):
        chunk = None
        for t in range(3):
            value = q1[pl.ds(8 + 2 * LON * n + t, 24, stride=3), :]
            value = pltpu.roll(value, FIELDS * SLOT * t, 1) if t > 0 else value
            chunk = value if chunk is None else jnp.where(third < t, chunk, value)
        back[24 * n:24 * n + 24] = chunk
        if n % 4 == 3:
            rows = pl.ds(24 * (n - 3), 96)
            sends.append(pltpu.make_async_copy(back.at[rows], out.at[rows], sems.at[n // 4]))
            sends[-1].start()
    for copy in sends:
        copy.wait()


def join_kernel(middle, weight, back, out, block, sems):
    lane8 = lanes_of(8)
    lane = lanes_of(12)

    def body(lat):
        place = (lane - 32 * lat) & 127
        polar = place < POLAR
        even = ((place % 12 < SHARE) & (place != POLAR)) | (place == 127)
        copies = []
        for f in range(FIELDS):
            rows = pl.ds(f * UNIT, UNIT)
            block[rows, :] = middle[rows, :]
            for level in range(LEVELS):
                base = 12 * GROUPS * level
                for t in range(3):
                    start = FIELDS * SLOT * t + SLOT * f
                    target = (lane8 - (start + 32 * lat)) & 127
                    parts = []
                    for k in range(0, 24, 8):
                        value = back[base + k:base + k + 8]
                        for n in range(1, 8):
                            value = jnp.where(target >= 12 * n, back[base + 24 * n + k:base + 24 * n + k + 8], value)
                        parts.append(jnp.where(target >= 112, back[base + k:base + k + 8], value))
                    acc = pltpu.roll(jnp.concatenate(parts, axis=0), (-start) % 128, 1)
                    value = jnp.where(even, acc[:12], acc[12:])
                    at = pl.ds(f * UNIT + t * STEP + level + 2 * LEVELS * lat, 12, stride=3 * STEP)
                    near = weight[pl.ds(level * (LON + 4) + t, 12, stride=3), :]
                    block[at, :] = jnp.where(polar, value, middle[at, :] + near * value)
            copies.append(pltpu.make_async_copy(block.at[rows], out.at[rows], sems.at[f]))
            copies[-1].start()
        for copy in copies:
            copy.wait()

    on_core(body)


VMEM = pl.BlockSpec(memory_space=pltpu.VMEM)
SMEM = pl.BlockSpec(memory_space=pltpu.SMEM)
ANY = pl.BlockSpec(memory_space=pl.ANY)


def call(kernel, name, specs, shapes, scratch, grant, flops, moved, out_specs=None):
    params = {} if grant is None else {"vmem_limit_bytes": grant * 2**20}
    return pl.pallas_call(
        kernel,
        name=name,
        in_specs=specs,
        out_specs=jax.tree.map(lambda _: VMEM, shapes) if out_specs is None else out_specs,
        out_shape=shapes,
        scratch_shapes=scratch,
        compiler_params=pltpu.CompilerParams(**params),
        cost_estimate=pl.CostEstimate(flops=flops, bytes_accessed=moved, transcendentals=0),
    )


def f32(*shape):
    return jax.ShapeDtypeStruct(shape, jnp.float32)


def on_device(state, cx, cy, cutoff):
    state, cx, cy = to_rows(state), to_rows(cx), to_rows(cy)
    results = (f32(RING, 24, 128), f32(UNITS * LON * LEVELS, 128), f32(2 * EDGE * UNITS, 128))
    chunks, window, edge = call(
        pack_kernel,
        "pack",
        [ANY] * 3,
        results,
        [
            pltpu.VMEM((UNITS * UNIT, 128), jnp.float32),
            pltpu.VMEM((LEVELS, 4, 24, 128), jnp.float32),
            pltpu.VMEM((LEVELS, 12, 24, 128), jnp.float32),
            *(pltpu.VMEM(result.shape, jnp.float32) for result in results),
            pltpu.SemaphoreType.DMA((UNITS + 6,)),
        ],
        None,
        4_000_000,
        2_000_000,
        (ANY,) * 3,
    )(state, cx, cy)
    chunks = lax.all_to_all(chunks, "lon", 0, 0, tiled=True)
    window = lax.ppermute(window, "lat", [(0, 1), (1, 0)])
    head, tail = call(
        edge_kernel, "edges", [VMEM] * 2, (f32(EDGE * UNITS, 128),) * 2, [], 4, 100_000, 1_000_000
    )(edge, window)
    west = lax.ppermute(tail, "lon", [(i, (i + 1) % RING) for i in range(RING)])
    east = lax.ppermute(head, "lon", [((i + 1) % RING, i) for i in range(RING)])
    table = jnp.asarray(hartley_tables())
    limits = call(
        limit_kernel,
        "limits",
        [ANY, ANY, SMEM],
        jax.ShapeDtypeStruct((8, 128), jnp.int32),
        [],
        4,
        100_000,
        1_000_000,
    )(head, table, cutoff)
    back = call(
        circle_kernel,
        "circle",
        [VMEM] * 3 + [ANY] * 2,
        f32(RING * 12, 128),
        [
            pltpu.VMEM((RING * 12, 128), jnp.float32),
            pltpu.VMEM((NLON + 16, 128), jnp.float32),
            pltpu.VMEM((NLON + 16, 128), jnp.float32),
            pltpu.VMEM((5, NLON, 128), jnp.float32),
            pltpu.VMEM((NLON + 8, 256), jnp.float32),
            *(pltpu.VMEM((rows, 256), jnp.bfloat16) for rows in (NLON, HALF, HALF)),
            *(pltpu.VMEM((rows, 256), jnp.float32) for rows in (HALF, QUARTER, QUARTER)),
            pltpu.VMEM((NLON, 256), jnp.bfloat16),
            pltpu.SemaphoreType.DMA((4,)),
        ],
        24,
        1_000_000_000,
        6_000_000,
        ANY,
    )(chunks, table, limits, west, east)
    middle, weight = call(
        middle_kernel,
        "middle",
        [VMEM] * 6,
        (f32(FIELDS * UNIT, 128), f32(LEVELS * (LON + 4), 128)),
        [pltpu.VMEM((LON + 4, LAT + 128), jnp.float32), pltpu.VMEM((5, LON + 4, LAT + 128), jnp.float32)],
        8,
        20_000_000,
        3_000_000,
    )(state, cx, cy, west, east, window)
    back = lax.all_to_all(back.reshape(RING, 3, 4, 128), "lon", 0, 0, tiled=True).reshape(RING * 12, 128)
    out = call(
        join_kernel,
        "join",
        [VMEM] * 3,
        f32(FIELDS * UNIT, 128),
        [pltpu.VMEM((FIELDS * UNIT, 128), jnp.float32), pltpu.SemaphoreType.DMA((FIELDS,))],
        6,
        4_000_000,
        2_000_000,
        ANY,
    )(middle, weight, back)
    return from_rows(out)


def solution(mesh):
    return jax.shard_map(
        on_device,
        mesh=mesh,
        in_specs=(
            P(None, "lev", "lon", "lat"),
            P("lev", "lon", "lat"),
            P("lev", "lon", "lat"),
            P(),
        ),
        out_specs=P(None, "lev", "lon", "lat"),
        check_vma=False,
    )
```

time: 489 us -> 54.1 us (0.11); the launches traced: 482 us -> 53.8 us
  local copies, waits for them, and re-layouts: 195 us -> 1.61 us
  matrix products: 109 us -> 0 us
  other arithmetic: 56.5 us -> 0 us
  blocking collectives: 51.4 us -> 0 us
  waiting for transfers between devices: 38.6 us -> 17.7 us
  Pallas kernels: 0 us -> 13.1 us
  starting transfers between devices: 31.1 us -> 21.2 us
    dot_general x8 -> x0, matrix products: 109 us -> none  [the longest x2 27.8 us: filter_circles(): jnp.einsum('flrk,ik->flir', cosine * keep, costab, precision=highest)]
    unnamed x56 -> x12, local copies, waits for them, and re-layouts: 89.3 us -> 1.61 us
    all_to_all x2 -> x0, blocking collectives: 51.4 us -> none  [the longest x1 26.8 us: filter_circles(): lax.all_to_all(block, 'lon', split_axis=3, concat_axis=2, tiled=True)]
    all_to_all x9 -> x0, local copies, waits for them, and re-layouts: 33.5 us -> none  [the longest x4 21.7 us: filter_circles(): lax.all_to_all(filtered, 'lon', split_axis=2, concat_axis=3, tiled=True)]
    all_to_all x2, waiting for transfers between devices: 38.6 us -> 10.7 us  [the longest x1 9.33 us: on_device(): lax.all_to_all(back.reshape(RING, 3, 4, 128), 'lon', 0, 0, tiled=True)]
    add x4 -> x0, other arithmetic: 25.3 us -> none  [the longest x2 14.2 us: advance(): state + flux_west - flux_east + flux_south - flux_north + KAPPA * spread]
    add x5 -> x0, local copies, waits for them, and re-layouts: 21.2 us -> none  [the longest x2 14.7 us: filter_circles(): result + jnp.einsum('flrk,ik->flir', sine * keep, sintab, precision=highest)]
    mul x10 -> x0, local copies, waits for them, and re-layouts: 20.7 us -> none  [the longest x3 5.07 us: advance(): jnp.maximum(south_face, 0.0) * south + jnp.minimum(south_face, 0.0) * state]
  transfers between devices with their start and end apart: 12 -> 5, of which waited for: 2 -> 4; matrix products, arithmetic and copies ran while one was open for 11% -> 0% of each run, Pallas kernels for 0% -> 5%
where the time goes in v1:
time: 54.1 us; the launch traced here: 53.8 us
  starting transfers between devices  21.2 us (39%)
  waiting for transfers between devices  17.7 us (33%)
  Pallas kernels  13.1 us (24%)
  local copies, waits for them, and re-layouts  1.61 us (3%)
    all_to_all x1, starting transfers between devices, on_device(): chunks = lax.all_to_all(chunks, 'lon', 0, 0, tiled=True)  11.4 us
    all_to_all x1, waiting for transfers between devices, on_device(): lax.all_to_all(back.reshape(RING, 3, 4, 128), 'lon', 0, 0, tiled=True)  9.33 us
    pallas_call x1, Pallas kernels, on_device(): call(circle_kernel, 'circle', [VMEM] * 3 + [ANY] * 2, f32(RING * 12, 128)...  6.82 us
    ppermute x1, waiting for transfers between devices, on_device(): west = lax.ppermute(tail, 'lon', [(i, (i + 1) % RING) for i in range(RING)])  5.23 us
    all_to_all x1, starting transfers between devices, on_device(): lax.all_to_all(back.reshape(RING, 3, 4, 128), 'lon', 0, 0, tiled=True)  4.27 us
    ppermute x1, starting transfers between devices, on_device(): east = lax.ppermute(head, 'lon', [((i + 1) % RING, i) for i in range(RING)])  3.62 us
    pallas_call x1, Pallas kernels, on_device(): call(pack_kernel, 'pack', [ANY] * 3, results, [pltpu.VMEM((UNITS * UNIT,...  2.69 us
    pallas_call x1, Pallas kernels, on_device(): call(middle_kernel, 'middle', [VMEM] * 6, (f32(FIELDS * UNIT, 128), f32(L...  1.95 us
  transfers between devices with their start and end apart: 5, of which 4 were waited for; matrix products, arithmetic and copies ran while one was open for 0% of the time, Pallas kernels for 5%

profile of v1, /device:TPU:8, one launch (start us, length us, event | category | flops | bytes accessed | tf_op | source)
XLA Modules:
  0.0 53.8 jit_solution(16050878196341974337)
XLA Ops:
  0.0 0.0 copy-start.1
  0.0 2.7 %pack.1 = (f32[32,24,128]{2,1,0:T(8,128)}, f32[576,128]{1,0:T(8,128)}, f32[256,128]{1,0:T(8,128)}) custom-call(f32[1296,128]{1,0:T(8,128)} %bitcast.34, f32[216,128]{1,0:T(8,128)} %bitcast.37, f32[216,128]{1,0:T(8,128)} %bitcast.39), custom_call_target="tpu_custom_call" | custom-call | flops 4000000 | bytes 2000000 | tf_op jit(solution)/shard_map/pack/pallas_call | solution.py:414
  2.7 11.4 %all-to-all-start = ((f32[32,24,128]{2,1,0:T(8,128)}), f32[32,24,128]{2,1,0:T(8,128)}, u32[]{:S(2)}, u32[]{:S(2)}) async-start(f32[32,24,128]{2,1,0:T(8,128)} %get-tuple-element.18), calls=%async_computation | async-start | bytes 786432 | tf_op jit(solution)/shard_map/all_to_all | solution.py:431
  14.1 0.1 collective-permute-start
  14.2 1.8 %collective-permute-done.window = f32[576,128]{1,0:T(8,128)S(1)} collective-permute-done((f32[576,128]{1,0:T(8,128)}, f32[576,128]{1,0:T(8,128)S(1)}, u32[]{:S(2)}, u32[]{:S(2)}) %collective-permute-start) | collective-permute-done | bytes 294944 | tf_op jit(solution)/shard_map/ppermute | solution.py:432
  16.0 0.0 copy-start.4
  16.0 0.9 %copy-done.4 = f32[256,128]{1,0:T(8,128)S(1)} copy-done((f32[256,128]{1,0:T(8,128)S(1)}, f32[256,128]{1,0:T(8,128)}, u32[]{:S(2)}) %copy-start.4) | copy-done | bytes 131096
  16.9 1.8 %collective-permute-start.1 = (f32[128,128]{1,0:T(8,128)S(1)}, f32[128,128]{1,0:T(8,128)S(1)}, u32[]{:S(2)}, u32[]{:S(2)}) collective-permute-start(f32[128,128]{1,0:T(8,128)S(1)} %get-tuple-element.14), channel_id=1, source_target_pairs={{0,8},{8,16},{16,24},{24,32},{32,40},{40,48},{48,56},{56,64},{64,7... | collective-permute-start | bytes 196616 | tf_op jit(solution)/shard_map/ppermute | solution.py:436
  18.8 3.6 %collective-permute-start.2 = (f32[128,128]{1,0:T(8,128)S(1)}, f32[128,128]{1,0:T(8,128)S(1)}, u32[]{:S(2)}, u32[]{:S(2)}) collective-permute-start(f32[128,128]{1,0:T(8,128)S(1)} %get-tuple-element.15.head), channel_id=1, source_target_pairs={{8,0},{16,8},{24,16},{32,24},{40,32},{48,40},{56,48},{64,56},{72,6... | collective-permute-start | bytes 196616 | tf_op jit(solution)/shard_map/ppermute | solution.py:437
  22.4 0.0 copy-done.1
  22.4 0.0 copy-start.5
  22.4 0.7 %copy-done.5 = s32[768]{0:T(1024)S(1)} copy-done((s32[768]{0:T(1024)S(1)}, s32[768]{0:T(1024)}, u32[]{:S(2)}) %copy-start.5) | copy-done | bytes 3096
  23.1 0.6 %limits.1 = s32[8,128]{1,0:T(8,128)S(1)} custom-call(f32[128,128]{1,0:T(8,128)S(1)} %get-tuple-element.15.head, bf16[576,1728]{1,0:T(8,128)(2,1)S(1)} %copy-done.1, s32[768]{0:T(1024)S(1)} %copy-done.5), custom_call_target="tpu_custom_call" | custom-call | flops 100000 | bytes 1000000 | tf_op jit(solution)/shard_map/limits/pallas_call | solution.py:439
  23.7 0.0 copy-start
  23.7 0.0 copy-start.2
  23.7 0.0 copy-start.3
  23.7 5.2 %collective-permute-done.1.west = f32[128,128]{1,0:T(8,128)S(1)} collective-permute-done((f32[128,128]{1,0:T(8,128)S(1)}, f32[128,128]{1,0:T(8,128)S(1)}, u32[]{:S(2)}, u32[]{:S(2)}) %collective-permute-start.1) | collective-permute-done | bytes 65568 | tf_op jit(solution)/shard_map/ppermute | solution.py:436
  29.0 0.0 collective-permute-done.2.east
  29.0 1.4 %all-to-all-done.chunks = f32[32,24,128]{2,1,0:T(8,128)} async-done(((f32[32,24,128]{2,1,0:T(8,128)}), f32[32,24,128]{2,1,0:T(8,128)}, u32[]{:S(2)}, u32[]{:S(2)}) %all-to-all-start) | async-done | bytes 393248 | tf_op jit(solution)/shard_map/all_to_all | solution.py:431
  30.3 6.8 %circle.1 = f32[384,128]{1,0:T(8,128)} custom-call(f32[32,24,128]{2,1,0:T(8,128)} %all-to-all-done.chunks, bf16[576,1728]{1,0:T(8,128)(2,1)S(1)} %copy-done.1, s32[8,128]{1,0:T(8,128)S(1)} %limits.1, f32[128,128]{1,0:T(8,128)S(1)} %collective-permute-done.1.west, f32[128,128]{1,0:T(8,128)S(1)} %collective-permute-done.2.east), custom_call_target="tpu_custom_call" | custom-call | flops 1000000000 | bytes 6000000 | tf_op jit(solution)/shard_map/circle/pallas_call | solution.py:449
  37.2 4.3 %all-to-all-start.1 = ((f32[32,3,4,128]{3,2,1,0:T(4,128)}), f32[32,3,4,128]{3,2,1,0:T(4,128)S(1)}, u32[]{:S(2)}, u32[]{:S(2)}) async-start(f32[32,3,4,128]{3,2,1,0:T(4,128)} %bitcast.25), calls=%async_computation.1 | async-start | bytes 393216 | tf_op jit(solution)/shard_map/all_to_all | solution.py:480
  41.4 0.0 copy-done
  41.5 0.0 copy-done.2
  41.5 0.0 copy-done.3
  41.5 2.0 %middle.1 = (f32[1296,128]{1,0:T(8,128)S(1)}, f32[80,128]{1,0:T(8,128)S(1)}) custom-call(f32[1296,128]{1,0:T(8,128)S(1)} %bitcast.35, f32[216,128]{1,0:T(8,128)S(1)} %bitcast.38, f32[216,128]{1,0:T(8,128)S(1)} %bitcast.40, f32[128,128]{1,0:T(8,128)S(1)} %collective-permute-done.1.west, f32[128,128]{1,0:T(8,128)S(1)} %collective-permute-done.2.east, ...), custom_call_target="tpu_custom_call" | custom-call | flops 20000000 | bytes 3000000 | tf_op jit(solution)/shard_map/middle/pallas_call | solution.py:470
  43.4 9.3 %all-to-all-done.1 = f32[32,3,4,128]{3,2,1,0:T(4,128)S(1)} async-done(((f32[32,3,4,128]{3,2,1,0:T(4,128)}), f32[32,3,4,128]{3,2,1,0:T(4,128)S(1)}, u32[]{:S(2)}, u32[]{:S(2)}) %all-to-all-start.1) | async-done | bytes 196640 | tf_op jit(solution)/shard_map/all_to_all | solution.py:480
  52.8 1.0 %join.1 = f32[1296,128]{1,0:T(8,128)} custom-call(f32[1296,128]{1,0:T(8,128)S(1)} %get-tuple-element.16.middle, f32[80,128]{1,0:T(8,128)S(1)} %get-tuple-element.17.weight, f32[384,128]{1,0:T(8,128)S(1)} %bitcast.36), custom_call_target="tpu_custom_call" | custom-call | flops 4000000 | bytes 2000000 | tf_op jit(solution)/shard_map/join/pallas_call | solution.py:481
  (1 shorter events, 0.0 us)
Async XLA Ops:
  0.0 22.4 %copy-start.1 = (bf16[576,1728]{1,0:T(8,128)(2,1)S(1)}, bf16[576,1728]{1,0:T(8,128)(2,1)}, u32[]{:S(2)}) copy-start(bf16[576,1728]{1,0:T(8,128)(2,1)} %constant.2.clone.table) | copy-start | bytes 5971972
  2.7 27.6 %all-to-all-start = ((f32[32,24,128]{2,1,0:T(8,128)}), f32[32,24,128]{2,1,0:T(8,128)}, u32[]{:S(2)}, u32[]{:S(2)}) async-start(f32[32,24,128]{2,1,0:T(8,128)} %get-tuple-element.18), calls=%async_computation | async-start | bytes 786432 | tf_op jit(solution)/shard_map/all_to_all | solution.py:431
  14.1 1.9 %collective-permute-start = (f32[576,128]{1,0:T(8,128)}, f32[576,128]{1,0:T(8,128)S(1)}, u32[]{:S(2)}, u32[]{:S(2)}) collective-permute-start(f32[576,128]{1,0:T(8,128)} %get-tuple-element.13), channel_id=1, source_target_pairs={{0,4},{4,0},{1,5},{5,1},{2,6},{6,2},{3,7},{7,3},{8,12},{12,8},{9,1... | collective-permute-start | bytes 884744 | tf_op jit(solution)/shard_map/ppermute | solution.py:432
  16.0 0.9 %copy-start.4 = (f32[256,128]{1,0:T(8,128)S(1)}, f32[256,128]{1,0:T(8,128)}, u32[]{:S(2)}) copy-start(f32[256,128]{1,0:T(8,128)} %get-tuple-element.12.edge) | copy-start | bytes 393220
  16.9 12.0 %collective-permute-start.1 = (f32[128,128]{1,0:T(8,128)S(1)}, f32[128,128]{1,0:T(8,128)S(1)}, u32[]{:S(2)}, u32[]{:S(2)}) collective-permute-start(f32[128,128]{1,0:T(8,128)S(1)} %get-tuple-element.14), channel_id=1, source_target_pairs={{0,8},{8,16},{16,24},{24,32},{32,40},{40,48},{48,56},{56,64},{64,7... | collective-permute-start | bytes 196616 | tf_op jit(solution)/shard_map/ppermute | solution.py:436
  18.8 10.2 %collective-permute-start.2 = (f32[128,128]{1,0:T(8,128)S(1)}, f32[128,128]{1,0:T(8,128)S(1)}, u32[]{:S(2)}, u32[]{:S(2)}) collective-permute-start(f32[128,128]{1,0:T(8,128)S(1)} %get-tuple-element.15.head), channel_id=1, source_target_pairs={{8,0},{16,8},{24,16},{32,24},{40,32},{48,40},{56,48},{64,56},{72,6... | collective-permute-start | bytes 196616 | tf_op jit(solution)/shard_map/ppermute | solution.py:437
  22.4 0.7 %copy-start.5 = (s32[768]{0:T(1024)S(1)}, s32[768]{0:T(1024)}, u32[]{:S(2)}) copy-start(s32[768]{0:T(1024)} %cutoff.1) | copy-start | bytes 9220
  23.7 17.8 %copy-start = (f32[6,2,36,384]{3,1,2,0:T(2,128)S(1)}, f32[6,2,36,384]{3,1,2,0:T(2,128)}, u32[]{:S(2)}) copy-start(f32[6,2,36,384]{3,1,2,0:T(2,128)} %param.5) | copy-start | bytes 1990660
  23.7 17.8 %copy-start.2 = (f32[2,36,384]{2,0,1:T(2,128)S(1)}, f32[2,36,384]{2,0,1:T(2,128)}, u32[]{:S(2)}) copy-start(f32[2,36,384]{2,0,1:T(2,128)} %param.6) | copy-start | bytes 331780
  23.7 17.8 %copy-start.3 = (f32[2,36,384]{2,0,1:T(2,128)S(1)}, f32[2,36,384]{2,0,1:T(2,128)}, u32[]{:S(2)}) copy-start(f32[2,36,384]{2,0,1:T(2,128)} %param.7) | copy-start | bytes 331780
  37.2 15.6 %all-to-all-start.1 = ((f32[32,3,4,128]{3,2,1,0:T(4,128)}), f32[32,3,4,128]{3,2,1,0:T(4,128)S(1)}, u32[]{:S(2)}, u32[]{:S(2)}) async-start(f32[32,3,4,128]{3,2,1,0:T(4,128)} %bitcast.25), calls=%async_computation.1 | async-start | bytes 393216 | tf_op jit(solution)/shard_map/all_to_all | solution.py:480

commit v2 on v1

--- a/solution.py
+++ b/solution.py
@@ -279,29 +279,38 @@
         wave = step * (lax.broadcasted_iota(jnp.int32, (PIECE, 128), 0) + at) + shift
         return jnp.where(jnp.minimum(wave, NLON - wave) <= limit, 1.0 / NLON, 0.0)
 
-    def products():
-        odd_out[...] = jnp.dot(table[:, :NLON], odd_in[...], preferred_element_type=jnp.float32)
-        even_out[...] = jnp.dot(table[:QUARTER, NLON:], even_in[...], preferred_element_type=jnp.float32)
-        rest_out[...] = jnp.dot(table[QUARTER:, NLON:], rest_in[...], preferred_element_type=jnp.float32)
+    parts = {
+        "odd": (odd_in, odd_out, HALF, (2, 1), (slice(None), slice(0, NLON))),
+        "even": (even_in, even_out, QUARTER, (4, 0), (slice(0, QUARTER), slice(NLON, None))),
+        "rest": (rest_in, rest_out, QUARTER, (4, 2), (slice(QUARTER, None), slice(NLON, None))),
+    }
+
+    def product(name):
+        source, target, _, _, place = parts[name]
+        target[...] = jnp.dot(table[place], source[...], preferred_element_type=jnp.float32)
+
+    def cut(name):
+        source, target, count, waves, _ = parts[name]
+        for b in range(0, count, PIECE):
+            split(source, b, result(target, b) * kept(b, *waves), count)
 
     def result(ref, at):
         return ref[at:at + PIECE, :128] + ref[at:at + PIECE, 128:]
 
     def filtered(q, finish):
+        for b in range(0, HALF, PIECE):
+            split(odd_in, b, q[8 + b:8 + b + PIECE] - q[8 + HALF + b:8 + HALF + b + PIECE], HALF)
+        product("odd")
         for b in range(0, QUARTER, PIECE):
             x = [q[8 + QUARTER * n + b:8 + QUARTER * n + b + PIECE] for n in range(4)]
-            split(odd_in, b, x[0] - x[2], HALF)
-            split(odd_in, QUARTER + b, x[1] - x[3], HALF)
             here, there = x[0] + x[2], x[1] + x[3]
             split(even_in, b, here + there, QUARTER)
             split(rest_in, b, here - there, QUARTER)
-        products()
-        for b in range(0, HALF, PIECE):
-            split(odd_in, b, result(odd_out, b) * kept(b, 2, 1), HALF)
-        for b in range(0, QUARTER, PIECE):
-            split(even_in, b, result(even_out, b) * kept(b, 4, 0), QUARTER)
-            split(rest_in, b, result(rest_out, b) * kept(b, 4, 2), QUARTER)
-        products()
+        product("even")
+        product("rest")
+        for name in parts:
+            cut(name)
+            product(name)
         for b in range(0, QUARTER, PIECE):
             odd = result(odd_out, b), result(odd_out, QUARTER + b)
             even, rest = result(even_out, b), result(rest_out, b)

time: 54.1 us -> 54.1 us (level)
  no operation moved by 1% of the time
where the time goes in v2:
time: 54.1 us; the launch traced here: 53.8 us
  starting transfers between devices  21.2 us (39%)
  waiting for transfers between devices  17.7 us (33%)
  Pallas kernels  13.1 us (24%)
  local copies, waits for them, and re-layouts  1.61 us (3%)
    all_to_all x1, starting transfers between devices, on_device(): chunks = lax.all_to_all(chunks, 'lon', 0, 0, tiled=True)  11.4 us
    all_to_all x1, waiting for transfers between devices, on_device(): lax.all_to_all(back.reshape(RING, 3, 4, 128), 'lon', 0, 0, tiled=True)  9.33 us
    pallas_call x1, Pallas kernels, on_device(): call(circle_kernel, 'circle', [VMEM] * 3 + [ANY] * 2, f32(RING * 12, 128)...  6.79 us
    ppermute x1, waiting for transfers between devices, on_device(): west = lax.ppermute(tail, 'lon', [(i, (i + 1) % RING) for i in range(RING)])  5.23 us
    all_to_all x1, starting transfers between devices, on_device(): lax.all_to_all(back.reshape(RING, 3, 4, 128), 'lon', 0, 0, tiled=True)  4.27 us
    ppermute x1, starting transfers between devices, on_device(): east = lax.ppermute(head, 'lon', [((i + 1) % RING, i) for i in range(RING)])  3.62 us
    pallas_call x1, Pallas kernels, on_device(): call(pack_kernel, 'pack', [ANY] * 3, results, [pltpu.VMEM((UNITS * UNIT,...  2.69 us
    pallas_call x1, Pallas kernels, on_device(): call(middle_kernel, 'middle', [VMEM] * 6, (f32(FIELDS * UNIT, 128), f32(L...  1.95 us
  transfers between devices with their start and end apart: 5, of which 4 were waited for; matrix products, arithmetic and copies ran while one was open for 0% of the time, Pallas kernels for 5%

profile of v2, /device:TPU:8, one launch (start us, length us, event | category | flops | bytes accessed | tf_op | source)
XLA Modules:
  0.0 53.8 jit_solution(11363991296688003400)
XLA Ops:
  0.0 0.0 copy-start.1
  0.0 2.7 %pack.1 = (f32[32,24,128]{2,1,0:T(8,128)}, f32[576,128]{1,0:T(8,128)}, f32[256,128]{1,0:T(8,128)}) custom-call(f32[1296,128]{1,0:T(8,128)} %bitcast.34, f32[216,128]{1,0:T(8,128)} %bitcast.37, f32[216,128]{1,0:T(8,128)} %bitcast.39), custom_call_target="tpu_custom_call" | custom-call | flops 4000000 | bytes 2000000 | tf_op jit(solution)/shard_map/pack/pallas_call | solution.py:423
  2.7 11.4 %all-to-all-start = ((f32[32,24,128]{2,1,0:T(8,128)}), f32[32,24,128]{2,1,0:T(8,128)}, u32[]{:S(2)}, u32[]{:S(2)}) async-start(f32[32,24,128]{2,1,0:T(8,128)} %get-tuple-element.18), calls=%async_computation | async-start | bytes 786432 | tf_op jit(solution)/shard_map/all_to_all | solution.py:440
  14.1 0.1 collective-permute-start
  14.2 1.8 %collective-permute-done.window = f32[576,128]{1,0:T(8,128)S(1)} collective-permute-done((f32[576,128]{1,0:T(8,128)}, f32[576,128]{1,0:T(8,128)S(1)}, u32[]{:S(2)}, u32[]{:S(2)}) %collective-permute-start) | collective-permute-done | bytes 294944 | tf_op jit(solution)/shard_map/ppermute | solution.py:441
  16.0 0.0 copy-start.4
  16.0 0.9 %copy-done.4 = f32[256,128]{1,0:T(8,128)S(1)} copy-done((f32[256,128]{1,0:T(8,128)S(1)}, f32[256,128]{1,0:T(8,128)}, u32[]{:S(2)}) %copy-start.4) | copy-done | bytes 131096
  16.9 1.8 %collective-permute-start.1 = (f32[128,128]{1,0:T(8,128)S(1)}, f32[128,128]{1,0:T(8,128)S(1)}, u32[]{:S(2)}, u32[]{:S(2)}) collective-permute-start(f32[128,128]{1,0:T(8,128)S(1)} %get-tuple-element.14), channel_id=1, source_target_pairs={{0,8},{8,16},{16,24},{24,32},{32,40},{40,48},{48,56},{56,64},{64,7... | collective-permute-start | bytes 196616 | tf_op jit(solution)/shard_map/ppermute | solution.py:445
  18.8 3.6 %collective-permute-start.2 = (f32[128,128]{1,0:T(8,128)S(1)}, f32[128,128]{1,0:T(8,128)S(1)}, u32[]{:S(2)}, u32[]{:S(2)}) collective-permute-start(f32[128,128]{1,0:T(8,128)S(1)} %get-tuple-element.15.head), channel_id=1, source_target_pairs={{8,0},{16,8},{24,16},{32,24},{40,32},{48,40},{56,48},{64,56},{72,6... | collective-permute-start | bytes 196616 | tf_op jit(solution)/shard_map/ppermute | solution.py:446
  22.4 0.0 copy-done.1
  22.4 0.0 copy-start.5
  22.4 0.7 %copy-done.5 = s32[768]{0:T(1024)S(1)} copy-done((s32[768]{0:T(1024)S(1)}, s32[768]{0:T(1024)}, u32[]{:S(2)}) %copy-start.5) | copy-done | bytes 3096
  23.1 0.6 %limits.1 = s32[8,128]{1,0:T(8,128)S(1)} custom-call(f32[128,128]{1,0:T(8,128)S(1)} %get-tuple-element.15.head, bf16[576,1728]{1,0:T(8,128)(2,1)S(1)} %copy-done.1, s32[768]{0:T(1024)S(1)} %copy-done.5), custom_call_target="tpu_custom_call" | custom-call | flops 100000 | bytes 1000000 | tf_op jit(solution)/shard_map/limits/pallas_call | solution.py:448
  23.7 0.0 copy-start
  23.7 0.0 copy-start.2
  23.7 0.0 copy-start.3
  23.7 5.2 %collective-permute-done.1.west = f32[128,128]{1,0:T(8,128)S(1)} collective-permute-done((f32[128,128]{1,0:T(8,128)S(1)}, f32[128,128]{1,0:T(8,128)S(1)}, u32[]{:S(2)}, u32[]{:S(2)}) %collective-permute-start.1) | collective-permute-done | bytes 65568 | tf_op jit(solution)/shard_map/ppermute | solution.py:445
  29.0 0.0 collective-permute-done.2.east
  29.0 1.4 %all-to-all-done.chunks = f32[32,24,128]{2,1,0:T(8,128)} async-done(((f32[32,24,128]{2,1,0:T(8,128)}), f32[32,24,128]{2,1,0:T(8,128)}, u32[]{:S(2)}, u32[]{:S(2)}) %all-to-all-start) | async-done | bytes 393248 | tf_op jit(solution)/shard_map/all_to_all | solution.py:440
  30.3 6.8 %circle.1 = f32[384,128]{1,0:T(8,128)} custom-call(f32[32,24,128]{2,1,0:T(8,128)} %all-to-all-done.chunks, bf16[576,1728]{1,0:T(8,128)(2,1)S(1)} %copy-done.1, s32[8,128]{1,0:T(8,128)S(1)} %limits.1, f32[128,128]{1,0:T(8,128)S(1)} %collective-permute-done.1.west, f32[128,128]{1,0:T(8,128)S(1)} %collective-permute-done.2.east), custom_call_target="tpu_custom_call" | custom-call | flops 1000000000 | bytes 6000000 | tf_op jit(solution)/shard_map/circle/pallas_call | solution.py:458
  37.1 4.3 %all-to-all-start.1 = ((f32[32,3,4,128]{3,2,1,0:T(4,128)}), f32[32,3,4,128]{3,2,1,0:T(4,128)S(1)}, u32[]{:S(2)}, u32[]{:S(2)}) async-start(f32[32,3,4,128]{3,2,1,0:T(4,128)} %bitcast.25), calls=%async_computation.1 | async-start | bytes 393216 | tf_op jit(solution)/shard_map/all_to_all | solution.py:489
  41.4 0.0 copy-done
  41.4 0.0 copy-done.2
  41.4 0.0 copy-done.3
  41.4 2.0 %middle.1 = (f32[1296,128]{1,0:T(8,128)S(1)}, f32[80,128]{1,0:T(8,128)S(1)}) custom-call(f32[1296,128]{1,0:T(8,128)S(1)} %bitcast.35, f32[216,128]{1,0:T(8,128)S(1)} %bitcast.38, f32[216,128]{1,0:T(8,128)S(1)} %bitcast.40, f32[128,128]{1,0:T(8,128)S(1)} %collective-permute-done.1.west, f32[128,128]{1,0:T(8,128)S(1)} %collective-permute-done.2.east, ...), custom_call_target="tpu_custom_call" | custom-call | flops 20000000 | bytes 3000000 | tf_op jit(solution)/shard_map/middle/pallas_call | solution.py:479
  43.4 9.3 %all-to-all-done.1 = f32[32,3,4,128]{3,2,1,0:T(4,128)S(1)} async-done(((f32[32,3,4,128]{3,2,1,0:T(4,128)}), f32[32,3,4,128]{3,2,1,0:T(4,128)S(1)}, u32[]{:S(2)}, u32[]{:S(2)}) %all-to-all-start.1) | async-done | bytes 196640 | tf_op jit(solution)/shard_map/all_to_all | solution.py:489
  52.7 1.0 %join.1 = f32[1296,128]{1,0:T(8,128)} custom-call(f32[1296,128]{1,0:T(8,128)S(1)} %get-tuple-element.16.middle, f32[80,128]{1,0:T(8,128)S(1)} %get-tuple-element.17.weight, f32[384,128]{1,0:T(8,128)S(1)} %bitcast.36), custom_call_target="tpu_custom_call" | custom-call | flops 4000000 | bytes 2000000 | tf_op jit(solution)/shard_map/join/pallas_call | solution.py:490
  (1 shorter events, 0.0 us)
Async XLA Ops:
  0.0 22.4 %copy-start.1 = (bf16[576,1728]{1,0:T(8,128)(2,1)S(1)}, bf16[576,1728]{1,0:T(8,128)(2,1)}, u32[]{:S(2)}) copy-start(bf16[576,1728]{1,0:T(8,128)(2,1)} %constant.2.clone.table) | copy-start | bytes 5971972
  2.7 27.6 %all-to-all-start = ((f32[32,24,128]{2,1,0:T(8,128)}), f32[32,24,128]{2,1,0:T(8,128)}, u32[]{:S(2)}, u32[]{:S(2)}) async-start(f32[32,24,128]{2,1,0:T(8,128)} %get-tuple-element.18), calls=%async_computation | async-start | bytes 786432 | tf_op jit(solution)/shard_map/all_to_all | solution.py:440
  14.1 1.9 %collective-permute-start = (f32[576,128]{1,0:T(8,128)}, f32[576,128]{1,0:T(8,128)S(1)}, u32[]{:S(2)}, u32[]{:S(2)}) collective-permute-start(f32[576,128]{1,0:T(8,128)} %get-tuple-element.13), channel_id=1, source_target_pairs={{0,4},{4,0},{1,5},{5,1},{2,6},{6,2},{3,7},{7,3},{8,12},{12,8},{9,1... | collective-permute-start | bytes 884744 | tf_op jit(solution)/shard_map/ppermute | solution.py:441
  16.0 0.9 %copy-start.4 = (f32[256,128]{1,0:T(8,128)S(1)}, f32[256,128]{1,0:T(8,128)}, u32[]{:S(2)}) copy-start(f32[256,128]{1,0:T(8,128)} %get-tuple-element.12.edge) | copy-start | bytes 393220
  16.9 12.0 %collective-permute-start.1 = (f32[128,128]{1,0:T(8,128)S(1)}, f32[128,128]{1,0:T(8,128)S(1)}, u32[]{:S(2)}, u32[]{:S(2)}) collective-permute-start(f32[128,128]{1,0:T(8,128)S(1)} %get-tuple-element.14), channel_id=1, source_target_pairs={{0,8},{8,16},{16,24},{24,32},{32,40},{40,48},{48,56},{56,64},{64,7... | collective-permute-start | bytes 196616 | tf_op jit(solution)/shard_map/ppermute | solution.py:445
  18.8 10.2 %collective-permute-start.2 = (f32[128,128]{1,0:T(8,128)S(1)}, f32[128,128]{1,0:T(8,128)S(1)}, u32[]{:S(2)}, u32[]{:S(2)}) collective-permute-start(f32[128,128]{1,0:T(8,128)S(1)} %get-tuple-element.15.head), channel_id=1, source_target_pairs={{8,0},{16,8},{24,16},{32,24},{40,32},{48,40},{56,48},{64,56},{72,6... | collective-permute-start | bytes 196616 | tf_op jit(solution)/shard_map/ppermute | solution.py:446
  22.4 0.7 %copy-start.5 = (s32[768]{0:T(1024)S(1)}, s32[768]{0:T(1024)}, u32[]{:S(2)}) copy-start(s32[768]{0:T(1024)} %cutoff.1) | copy-start | bytes 9220
  23.7 17.7 %copy-start = (f32[6,2,36,384]{3,1,2,0:T(2,128)S(1)}, f32[6,2,36,384]{3,1,2,0:T(2,128)}, u32[]{:S(2)}) copy-start(f32[6,2,36,384]{3,1,2,0:T(2,128)} %param.5) | copy-start | bytes 1990660
  23.7 17.7 %copy-start.2 = (f32[2,36,384]{2,0,1:T(2,128)S(1)}, f32[2,36,384]{2,0,1:T(2,128)}, u32[]{:S(2)}) copy-start(f32[2,36,384]{2,0,1:T(2,128)} %param.6) | copy-start | bytes 331780
  23.7 17.7 %copy-start.3 = (f32[2,36,384]{2,0,1:T(2,128)S(1)}, f32[2,36,384]{2,0,1:T(2,128)}, u32[]{:S(2)}) copy-start(f32[2,36,384]{2,0,1:T(2,128)} %param.7) | copy-start | bytes 331780
  37.1 15.6 %all-to-all-start.1 = ((f32[32,3,4,128]{3,2,1,0:T(4,128)}), f32[32,3,4,128]{3,2,1,0:T(4,128)S(1)}, u32[]{:S(2)}, u32[]{:S(2)}) async-start(f32[32,3,4,128]{3,2,1,0:T(4,128)} %bitcast.25), calls=%async_computation.1 | async-start | bytes 393216 | tf_op jit(solution)/shard_map/all_to_all | solution.py:489
